TPU v7x, 256 devices: a whole 4x4x8 slice. The times are simulated.
256 devices in a mesh: dp: 8 (over z_lo, core), expert: 32 (over z_hi, y, x).
Axes of the slice: x: 4, y: 4, z: 8 (z_hi: 2, z_lo: 4; z = z_hi * 4 + z_lo), core: 2. Of those that a mesh axis runs over, the one named last changes fastest.
Arguments:
- tokens: bfloat16 [65536, 1280], P(('dp', 'expert')), may hold values from -24 to 24
- router: bfloat16 [1280, 64], replicated, may hold values from -11 to 11
- w_in: bfloat16 [64, 1280, 4096], P('expert', None, 'dp'), may hold values from -0.15625 to 0.15625
- w_out: bfloat16 [64, 4096, 1280], P('expert', 'dp'), may hold values from -0.09375 to 0.09375
- out_grad: bfloat16 [65536, 1280], P(('dp', 'expert')), may hold values from -6 to 6
Outputs:
- token_grad: bfloat16 [65536, 1280], P(('dp', 'expert'))
- router_grad: float32 [1280, 64], replicated
- w_in_grad: bfloat16 [64, 1280, 4096], P('expert', None, 'dp')
- w_out_grad: bfloat16 [64, 4096, 1280], P('expert', 'dp')
All inputs are finite; a program needn't handle non-finite values.
Results may differ from a plain program's by a relative error of at most 0.012.
Values may be sent and summed in bfloat16 or wider, within the bound.
A program may use at most 64 MiB of HBM per device.

v0:
```python
import jax
import jax.numpy as jnp
from jax import lax
from jax.sharding import Mesh
from jax.sharding import PartitionSpec as P

M = 256
DP = ("dp_0", "dp_1")
DP_EXPERT = ("dp_0", "dp_1", "expert")


def laid_out(blocks, dim):
    blocks = jnp.moveaxis(blocks, 0, dim)
    lengths = blocks.shape
    return blocks.reshape(*lengths[:dim], lengths[dim] * lengths[dim + 1], *lengths[dim + 2 :])


def gather_in_order(value, axes, order):
    blocks = value
    for k in order:
        blocks = lax.all_gather(blocks, axes[k])
    done = order[::-1]
    back = [done.index(k) for k in range(len(axes))]
    blocks = blocks.transpose(*back, *range(len(axes), blocks.ndim))
    return blocks.reshape(-1, *value.shape)


def gathered_by_axis(value, axes, order, dim):
    return laid_out(gather_in_order(value, axes, order), dim)


def activate(values):
    return jax.nn.gelu(values, approximate=True)


def to_experts(slot_rows):
    placed = lax.all_to_all(slot_rows, "expert", split_axis=1, concat_axis=0, tiled=True)
    return gathered_by_axis(placed, DP, (0, 1), 0)


def to_owners(partial_value):
    summed = lax.psum_scatter(partial_value, DP, scatter_dimension=0, tiled=True).astype(
        jnp.bfloat16
    )
    return lax.all_to_all(summed, "expert", split_axis=0, concat_axis=1, tiled=True)


def local(tokens, router, w_in, w_out, out_grad):
    images = tokens.shape[0] // M
    feature = tokens.shape[1]
    inputs = tokens.reshape(images, M, feature)
    grads = out_grad.reshape(images, M, feature)
    logits = jnp.einsum("bmd,de->bme", inputs, router, preferred_element_type=jnp.float32)
    dispatch = jax.nn.softmax(logits, axis=1)
    combine = jax.nn.softmax(logits, axis=2)
    dispatch_b = dispatch.astype(jnp.bfloat16)
    combine_b = combine.astype(jnp.bfloat16)
    slots = jnp.einsum(
        "bme,bmd->bed", dispatch_b, inputs, preferred_element_type=jnp.float32
    ).astype(jnp.bfloat16)
    slot_rows = to_experts(slots)
    hidden = jnp.einsum("red,edf->ref", slot_rows, w_in, preferred_element_type=jnp.float32)
    active, pull = jax.vjp(activate, hidden)
    active_b = active.astype(jnp.bfloat16)
    partial_value = jnp.einsum("ref,efd->red", active_b, w_out, preferred_element_type=jnp.float32)
    slot_out = to_owners(partial_value)
    slot_grad = jnp.einsum(
        "bme,bmd->bed", combine_b, grads, preferred_element_type=jnp.float32
    ).astype(jnp.bfloat16)
    grad_rows = to_experts(slot_grad)
    active_grad = jnp.einsum("red,efd->ref", grad_rows, w_out, preferred_element_type=jnp.float32)
    second_grad = jnp.einsum(
        "ref,red->efd", active_b, grad_rows, preferred_element_type=jnp.float32
    ).astype(jnp.bfloat16)
    hidden_grad = pull(active_grad)[0].astype(jnp.bfloat16)
    first_grad = jnp.einsum(
        "red,ref->edf", slot_rows, hidden_grad, preferred_element_type=jnp.float32
    ).astype(jnp.bfloat16)
    input_partial = jnp.einsum(
        "ref,edf->red", hidden_grad, w_in, preferred_element_type=jnp.float32
    )
    slot_in_grad = to_owners(input_partial)
    combine_grad = jnp.einsum("bmd,bed->bme", grads, slot_out, preferred_element_type=jnp.float32)
    dispatch_grad = jnp.einsum(
        "bmd,bed->bme", inputs, slot_in_grad, preferred_element_type=jnp.float32
    )
    logit_grad = combine * (combine_grad - jnp.sum(combine_grad * combine, axis=2, keepdims=True))
    logit_grad = logit_grad + dispatch * (
        dispatch_grad - jnp.sum(dispatch_grad * dispatch, axis=1, keepdims=True)
    )
    logit_b = logit_grad.astype(jnp.bfloat16)
    token_grad = jnp.einsum(
        "bme,bed->bmd", dispatch_b, slot_in_grad, preferred_element_type=jnp.float32
    )
    token_grad = token_grad + jnp.einsum(
        "bme,de->bmd", logit_b, router, preferred_element_type=jnp.float32
    )
    router_part = jnp.einsum("bmd,bme->de", inputs, logit_b, preferred_element_type=jnp.float32)
    router_grad = lax.psum(router_part, DP_EXPERT)
    return (
        token_grad.astype(jnp.bfloat16).reshape(images * M, feature),
        router_grad,
        first_grad,
        second_grad,
    )


def solution(mesh):
    split = Mesh(mesh.devices.reshape(4, 2, mesh.shape["expert"]), ("dp_0", "dp_1", "expert"))
    placed = (
        P(DP_EXPERT, None),
        P(),
        P("expert", None, DP),
        P("expert", DP, None),
        P(DP_EXPERT, None),
    )
    return jax.shard_map(
        local,
        mesh=split,
        in_specs=placed,
        out_specs=(P(DP_EXPERT, None), P(), P("expert", None, DP), P("expert", DP, None)),
        check_vma=False,
    )
```

profile of v0, /device:TPU:1, one launch (start us, length us, event | category | flops | bytes accessed | tf_op | source)
XLA Modules:
  0.0 484.6 jit_solution(391703074439383236)
XLA Ops:
  7.2 1.7 fusion.21
  11.3 1.6 reduce.16
  13.0 25.8 %all_to_all.42 = bf16[32,2,1280]{2,1,0:T(2,128)(2,1)S(1)} all-to-all(bf16[32,2,1280]{2,1,0:T(2,128)(2,1)S(1)} %reshape.119), channel_id=1, replica_groups=mesh['dp_0'=4,'dp_1'=2,'expert'=32] {'expert'}, dimensions={0} | all-to-all | bytes 327680 | tf_op jit(solution)/shard_map/all_to_all | solution.py:37
  39.9 15.2 %all_gather.23 = bf16[4,32,2,1280]{3,1,2,0:T(8,128)(2,1)} all-gather(bf16[1,32,2,1280]{3,1,2,0:T(8,128)(2,1)S(1)} %copy.33), channel_id=1, replica_groups=mesh['dp_0'=4,'dp_1'=2,'expert'=32] {'dp_0'}, dimensions={0}, use_global_device_ids=true | all-gather | bytes 819200 | tf_op jit(solution)/shard_map/all_gather | solution.py:21
  56.8 1.6 reduce.17
  58.5 15.0 %all_to_all.43 = bf16[32,2,1280]{2,1,0:T(2,128)(2,1)S(1)} all-to-all(bf16[32,2,1280]{2,1,0:T(2,128)(2,1)S(1)} %reshape.121), channel_id=1, replica_groups=mesh['dp_0'=4,'dp_1'=2,'expert'=32] {'expert'}, dimensions={0} | all-to-all | bytes 327680 | tf_op jit(solution)/shard_map/all_to_all | solution.py:37
  74.6 14.8 %all_gather.20 = bf16[4,32,2,1280]{3,1,2,0:T(8,128)(2,1)} all-gather(bf16[1,32,2,1280]{3,1,2,0:T(8,128)(2,1)S(1)} %copy.30), channel_id=1, replica_groups=mesh['dp_0'=4,'dp_1'=2,'expert'=32] {'dp_0'}, dimensions={0}, use_global_device_ids=true | all-gather | bytes 819200 | tf_op jit(solution)/shard_map/all_gather | solution.py:21
  89.5 2.5 copy.34
  92.0 15.6 %all-gather.5.cloned.1.call-done = bf16[8,32,2,1280]{3,1,2,0:T(8,128)(2,1)} async-done(((bf16[4,32,2,1280]{3,1,2,0:T(8,128)(2,1)}), bf16[8,32,2,1280]{3,1,2,0:T(8,128)(2,1)}) %all-gather.5.cloned.1.call-update) | async-done | bytes 1310736 | tf_op jit(solution)/shard_map/all_gather | solution.py:21
  110.1 1.6 copy-done.5
  113.8 2.4 convolution_bitcast_fusion.1
  116.3 4.5 convolution_bitcast_fusion
  120.8 4.1 convolution_convert_fusion
  124.9 32.3 %reduce-scatter.3.cloned.1.call-done = f32[32,2,1280]{2,0,1:T(8,128)} async-done(((f32[256,2,1280]{2,0,1:T(8,128)}), f32[32,2,1280]{2,0,1:T(8,128)}) %reduce-scatter.3.cloned.1.call-update) | async-done | bytes 327696 | tf_op jit(solution)/shard_map/reduce_scatter | solution.py:42
  159.0 11.1 %all-to-all-start.2 = ((bf16[32,2,1280]{2,1,0:T(2,128)(2,1)}), bf16[32,2,1280]{2,1,0:T(2,128)(2,1)S(1)}, u32[]{:S(2)}, u32[]{:S(2)}) async-start(bf16[32,2,1280]{2,1,0:T(2,128)(2,1)} %copy.35), calls=%async_computation.3 | async-start | bytes 327680 | tf_op jit(solution)/shard_map/all_to_all | solution.py:45
  170.1 3.9 convolution_convert_fusion.1
  174.0 29.4 %reduce-scatter.5.cloned.1.call-done = f32[32,2,1280]{2,0,1:T(8,128)} async-done(((f32[256,2,1280]{2,0,1:T(8,128)}), f32[32,2,1280]{2,0,1:T(8,128)}) %reduce-scatter.5.cloned.1.call-update) | async-done | bytes 327696 | tf_op jit(solution)/shard_map/reduce_scatter | solution.py:42
  205.3 10.4 %all-to-all-start.3 = ((bf16[32,2,1280]{2,1,0:T(2,128)(2,1)}), bf16[32,2,1280]{2,1,0:T(2,128)(2,1)}, u32[]{:S(2)}, u32[]{:S(2)}) async-start(bf16[32,2,1280]{2,1,0:T(2,128)(2,1)} %copy.36), calls=%async_computation.5 | async-start | bytes 327680 | tf_op jit(solution)/shard_map/all_to_all | solution.py:45
  219.1 7.9 %all-to-all-done.3 = bf16[32,2,1280]{2,1,0:T(2,128)(2,1)} async-done(((bf16[32,2,1280]{2,1,0:T(2,128)(2,1)}), bf16[32,2,1280]{2,1,0:T(2,128)(2,1)}, u32[]{:S(2)}, u32[]{:S(2)}) %all-to-all-start.3) | async-done | bytes 163872 | tf_op jit(solution)/shard_map/all_to_all | solution.py:45
  227.0 1.6 reshape.114
  230.9 1.9 convolution_bitcast_fusion.2
  232.8 2.7 fusion
  235.4 240.9 %all-reduce.2.cloned.1.call-done = f32[1280,64]{0,1:T(8,128)} async-done(((f32[1280,64]{0,1:T(8,128)}), f32[1280,64]{0,1:T(8,128)}) %all-reduce.2.cloned.1.call-update) | async-done | bytes 327696 | tf_op jit(solution)/shard_map/psum | solution.py:99
  476.3 1.7 copy.50
  (58 shorter events, 20.5 us)
Async XLA Ops:
  7.2 101.9 %copy-start = (bf16[2,1280,512]{2,1,0:T(8,128)(2,1)S(1)}, bf16[2,1280,512]{2,1,0:T(8,128)(2,1)}, u32[]{:S(2)}) copy-start(bf16[2,1280,512]{2,1,0:T(8,128)(2,1)} %param.7) | copy-start | bytes 7864324
  7.2 82.3 %all-gather.7.cloned.1.call-start = ((), (), s32[]{:S(2)}) async-start(), calls=%async_computation.10 | async-start | bytes 1966080 | tf_op jit(solution)/shard_map/all_gather | solution.py:21
  55.2 52.3 %all-gather.5.cloned.1.call-start = ((), (), s32[]{:S(2)}) async-start(), calls=%async_computation.9 | async-start | bytes 1966080 | tf_op jit(solution)/shard_map/all_gather | solution.py:21
  89.4 67.8 %reduce-scatter.3.cloned.1.call-start = ((), (), s32[]{:S(2)}) async-start(), calls=%async_computation.6 | async-start | bytes 2949120 | tf_op jit(solution)/shard_map/reduce_scatter | solution.py:42
  107.6 1.7 copy-start.1
  109.1 4.0 copy-start.4
  109.1 2.6 copy-start.5
  110.1 2.9 copy-start.3
  113.0 0.8 copy-start.6
  116.3 87.1 %reduce-scatter.5.cloned.1.call-start = ((), (), s32[]{:S(2)}) async-start(), calls=%async_computation.7 | async-start | bytes 2949120 | tf_op jit(solution)/shard_map/reduce_scatter | solution.py:42
  159.0 46.3 %all-to-all-start.2 = ((bf16[32,2,1280]{2,1,0:T(2,128)(2,1)}), bf16[32,2,1280]{2,1,0:T(2,128)(2,1)S(1)}, u32[]{:S(2)}, u32[]{:S(2)}) async-start(bf16[32,2,1280]{2,1,0:T(2,128)(2,1)} %copy.35), calls=%async_computation.3 | async-start | bytes 327680 | tf_op jit(solution)/shard_map/all_to_all | solution.py:45
  170.1 46.5 %copy-start.2 = (bf16[256,1280]{1,0:T(8,128)(2,1)S(1)}, bf16[256,1280]{1,0:T(8,128)(2,1)}, u32[]{:S(2)}) copy-start(bf16[256,1280]{1,0:T(8,128)(2,1)} %param.5) | copy-start | bytes 1966084
  205.3 10.4 %copy-start.8 = (bf16[32,2,1280]{2,1,0:T(2,128)(2,1)}, bf16[32,2,1280]{2,1,0:T(2,128)(2,1)S(1)}, u32[]{:S(2)}) copy-start(bf16[32,2,1280]{2,1,0:T(2,128)(2,1)S(1)} %all-to-all-done.2) | copy-start | bytes 491524
  205.3 21.8 %all-to-all-start.3 = ((bf16[32,2,1280]{2,1,0:T(2,128)(2,1)}), bf16[32,2,1280]{2,1,0:T(2,128)(2,1)}, u32[]{:S(2)}, u32[]{:S(2)}) async-start(bf16[32,2,1280]{2,1,0:T(2,128)(2,1)} %copy.36), calls=%async_computation.5 | async-start | bytes 327680 | tf_op jit(solution)/shard_map/all_to_all | solution.py:45
  215.6 260.7 %all-reduce.2.cloned.1.call-start = ((), (), s32[]{:S(2)}) async-start(), calls=%async_computation.8 | async-start | bytes 655360 | tf_op jit(solution)/shard_map/psum | solution.py:99
  219.1 13.6 %copy-start.7 = (bf16[1280,64]{0,1:T(8,128)(2,1)S(1)}, bf16[1280,64]{0,1:T(8,128)(2,1)}, u32[]{:S(2)}) copy-start(bf16[1280,64]{0,1:T(8,128)(2,1)} %param.6) | copy-start | bytes 491524
  230.3 0.6 copy-start.9
Sparse Core Ops, SparseCore 0:
  55.3 13.8 all-gather.6
  89.5 17.9 all-gather.4
  116.4 40.7 reduce-scatter.2
  159.6 43.8 reduce-scatter.4
  232.9 243.3 all-reduce.1
where the time goes:
time: 485 us
  waiting for transfers between devices  326 us (67%)
  blocking collectives  70.8 us (15%)
  matrix products  30 us (6%)
  starting transfers between devices  21.7 us (4%)
  local copies, waits for them, and re-layouts  16.6 us (3%)
  between operations  14 us (3%)
  other arithmetic  5.36 us (1%)
    psum x1, waiting for transfers between devices, local(): router_grad = lax.psum(router_part, DP_EXPERT)  241 us
    reduce_scatter x2, waiting for transfers between devices, to_owners(): lax.psum_scatter(partial_value, DP, scatter_dimension=0, tiled=True)  61.7 us
    all_to_all x2, blocking collectives, to_experts(): lax.all_to_all(slot_rows, 'expert', split_axis=1, concat_axis=0, tiled=True)  40.8 us
    all_gather x2, blocking collectives, gather_in_order(): blocks = lax.all_gather(blocks, axes[k])  30 us
    all_to_all x2, starting transfers between devices, to_owners(): lax.all_to_all(summed, 'expert', split_axis=0, concat_axis=1, tiled=True)  21.5 us
    all_gather x2, waiting for transfers between devices, gather_in_order(): blocks = lax.all_gather(blocks, axes[k])  15.6 us
  transfers between devices with their start and end apart: 7, of which 5 were waited for; matrix products, arithmetic and copies ran while one was open for 6% of the time, Pallas kernels for 0%

commit v1 on v0

v1 whole, which is shorter than its diff:
```python
import math

import jax
import jax.numpy as jnp
from jax import lax
from jax.experimental import pallas as pl
from jax.experimental.pallas import tpu as pltpu
from jax.sharding import PartitionSpec as P

MESH = pl.DeviceIdType.MESH
M, D, E, FS = 256, 1280, 64, 512
BF, F32 = jnp.bfloat16, jnp.float32
GELU_C, GELU_A = math.sqrt(2.0 / math.pi), 0.044715


def dot(a, b, ca=1, cb=0):
    return lax.dot_general(a, b, (((ca,), (cb,)), ((), ())), preferred_element_type=F32)


def perm(source, inverse):
    rows = lax.broadcasted_iota(jnp.int32, (128, 128), 1 if inverse else 0)
    cols = lax.broadcasted_iota(jnp.int32, (128, 128), 0 if inverse else 1)
    return (source(rows) == cols).astype(F32).astype(BF)


def reorder(matrix, rows):
    return dot(matrix, rows).astype(BF)


def kernel(
    x_ref, g_ref, r_ref, wi_hbm, wo_hbm,
    tg_ref, rg_ref, wig_hbm, wog_hbm,
    wi, wo, wig, wog,
    comb_v, disp_v,
    zs, zr, sv, rv, ob, relay, rows, act, hgv,
    p32, cs, cr, pv, ru, rd, fo, rl, zs2, zr2, sv2, rv2,
    ra, rb, rc, rp, zb, rf,
    wsem, osem, core_s, core_r, xs1, xr1, xs2, xr2,
    gr, gsu, gsd, gcs, gcr, pcs, pcr,
    rur, rdr, fr, rsu, rsd, as1, ar1, az_s, az_r, as2, ar2,
):
    dp, ex = lax.axis_index("dp"), lax.axis_index("expert")
    c, q = dp % 2, dp // 2
    h, xy = ex // 16, ex % 16
    y, x = xy // 4, xy % 4

    core_peer = (q * 2 + (1 - c), ex)
    xy_peers = []
    for d in range(1, 16):
        to = ((y + d // 4) % 4) * 4 + (x + d % 4) % 4
        frm = ((y + 4 - d // 4) % 4) * 4 + (x + 4 - d % 4) % 4
        xy_peers.append((d, to, frm))

    def z_dev(hh, qq):
        return (qq * 2 + c, hh * 16 + xy)

    barrier = pltpu.get_barrier_semaphore()

    def greet(dev):
        pl.semaphore_signal(barrier, inc=1, device_id=dev, device_id_type=MESH)

    greet(core_peer)
    for d, to, frm in xy_peers:
        greet((dp, h * 16 + to))
    z = h * 4 + q
    z_peers = []
    for d in range(1, 8):
        zt, zf = (z + d) % 8, (z + 8 - d) % 8
        z_peers.append((d, (zt % 4 * 2 + c, zt // 4 * 16 + xy), zf))
        greet(z_peers[-1][1])

    def remote(src, dst, ss, rs, dev):
        return pltpu.make_async_remote_copy(
            src_ref=src, dst_ref=dst, send_sem=ss, recv_sem=rs, device_id=dev, device_id_type=MESH
        )

    w_in_copy = pltpu.make_async_copy(wi_hbm, wi, wsem.at[0])
    w_out_copy = pltpu.make_async_copy(wo_hbm, wo, wsem.at[1])
    w_in_copy.start()
    w_out_copy.start()

    logits = dot(x_ref[...], r_ref[...])
    ed = jnp.exp(logits - jnp.max(logits, axis=0, keepdims=True))
    dispatch = ed / jnp.sum(ed, axis=0, keepdims=True)
    ec = jnp.exp(logits - jnp.max(logits, axis=1, keepdims=True))
    combine = ec / jnp.sum(ec, axis=1, keepdims=True)
    disp_v[...] = dispatch
    comb_v[...] = combine
    slots = dot(dispatch.astype(BF), x_ref[...], 0, 0).astype(BF)
    grads = dot(combine.astype(BF), g_ref[...], 0, 0).astype(BF)

    def order1(r):
        parity = jnp.where(r < 64, c, 1 - c)
        return ((r >> 5) & 1) * 64 + (r & 31) * 2 + parity

    def order2(r):
        half = jnp.where(((r >> 2) & 1) == 0, h, 1 - h)
        return (r & 1) * 64 + ((r >> 1) & 1) * 32 + half * 16 + (r >> 3)

    def order3(r):
        return ((r >> 1) & 15) * 8 + (r >> 5) * 2 + (r & 1)

    z1 = reorder(perm(order1, False), jnp.concatenate([slots, grads], axis=0))
    zs[...] = z1.reshape(2, 64, D)

    pl.semaphore_wait(barrier, 23)

    swap = remote(zs.at[1], zr, core_s.at[0], core_r.at[0], core_peer)
    swap.start()
    swap.wait()
    s1 = reorder(perm(order2, False), jnp.concatenate([zs[0], zr[...]], axis=0))
    sv[...] = s1.reshape(16, 8, D)

    def plane_exchange(src, dst, ss, rs):
        copies = []
        for d, to, frm in xy_peers:
            cp = remote(src.at[to], dst.at[xy], ss.at[d], rs.at[d], (dp, h * 16 + to))
            cp.start()
            copies.append(cp)
        dst[xy] = src[xy]
        return copies

    def finish(copies):
        for cp in copies:
            cp.wait()

    finish(plane_exchange(sv, rv, xs1, xr1))
    b1 = reorder(perm(order3, False), rv[...].reshape(128, D)).reshape(2, 2, 32, D)
    own = rows.at[1]
    for t in range(2):
        rows[1, t, q] = b1[0, t]
        ob[t] = b1[1, t]

    def g_copy(src, dst_idx, up, idx, qq):
        if up:
            dev = z_dev(h, qq + 1) if qq < 3 else z_dev(1 - h, 0)
        else:
            dev = z_dev(h, qq - 1) if qq > 0 else z_dev(1 - h, 3)
        dst = relay if dst_idx == 8 else own.at[:, dst_idx]
        sem = (gsu if up else gsd).at[idx]
        return remote(src, dst, sem, gr.at[dst_idx], dev)

    def g_recv(idx):
        dst = relay if idx == 8 else own.at[:, idx]
        remote(dst, dst, gsu.at[0], gr.at[idx], core_peer).wait_recv()

    def to_core(idx):
        return remote(own.at[:, idx], rows.at[0, :, idx], gcs.at[idx], gcr.at[idx], core_peer)

    def gather(qq, begin, events, last):
        sent = []

        def send(kind, up):
            if kind == "own":
                cp = g_copy(own.at[:, qq], qq, up, qq, qq)
            elif kind == "out":
                edge = (qq == 3 and up) or (qq == 0 and not up)
                cp = g_copy(ob, 4 + qq if edge else 8, up, 8, qq)
            elif kind == "relay":
                cp = g_copy(relay, 5 if qq == 0 else 6, up, 8 if qq == 3 else 7, qq)
            else:
                cp = g_copy(own.at[:, kind], kind, up, kind, qq)
            cp.start()
            sent.append(cp)

        for kind, up in begin:
            send(kind, up)
        cc = [to_core(qq)]
        cc[0].start()
        for idx, up in events:
            g_recv(idx)
            if up is not None:
                send("relay" if idx == 8 else idx, up)
            if idx != 8:
                cp = to_core(idx)
                cp.start()
                cc.append(cp)
        for cp in sent:
            cp.wait_send()
        for cp in cc:
            cp.wait()

    U, DN = True, False

    @pl.when(q == 0)
    def _():
        gather(0, [("own", U), ("out", DN)],
               [(7, U), (8, DN), (6, U), (1, None), (2, None), (3, None), (4, None), (5, None)], None)

    @pl.when(q == 1)
    def _():
        gather(1, [("out", DN), ("own", U), ("own", DN)],
               [(0, U), (2, DN), (7, U), (3, DN), (6, U), (4, DN), (5, DN)], None)

    @pl.when(q == 2)
    def _():
        gather(2, [("out", U), ("own", DN), ("own", U)],
               [(3, DN), (1, U), (4, DN), (0, U), (5, DN), (7, U), (6, U)], None)

    @pl.when(q == 3)
    def _():
        gather(3, [("own", DN), ("out", U)],
               [(4, DN), (8, U), (5, DN), (2, None), (1, None), (0, None), (7, None), (6, None)], None)

    w_in_copy.wait()
    w_out_copy.wait()

    def core_sum(t):
        return remote(cs.at[t], cr.at[t], pcs.at[t], pcr.at[t], core_peer)

    def expert(s, _):
        e = jnp.where(s == 1, c, 1 - c)
        hidden = dot(rows[s, 0].reshape(M, D), wi[e])
        inner = jnp.tanh(GELU_C * (hidden + GELU_A * hidden * hidden * hidden))
        cdf = 0.5 * (1.0 + inner)
        slope = cdf + hidden * (
            0.5 * (1.0 - inner * inner) * (GELU_C * (1.0 + 3.0 * GELU_A * hidden * hidden))
        )
        active = (hidden * cdf).astype(BF)
        act[s] = active
        out = dot(active, wo[e])

        @pl.when(s == 0)
        def _():
            cs[0] = out.astype(BF).reshape(8, 32, D)
            core_sum(0).start()

        @pl.when(s == 1)
        def _():
            p32[0] = out

        hg = (dot(rows[s, 1].reshape(M, D), wo[e], 1, 1) * slope).astype(BF)
        hgv[s] = hg
        back = dot(hg, wi[e], 1, 1)

        @pl.when(s == 0)
        def _():
            cs[1] = back.astype(BF).reshape(8, 32, D)
            core_sum(1).start()

        @pl.when(s == 1)
        def _():
            p32[1] = back

        return 0

    lax.fori_loop(0, 2, expert, 0)
    for t in range(2):
        core_sum(t).wait()
        pv[t] = (p32[t] + cr[t].reshape(M, D).astype(F32)).astype(BF).reshape(8, 32, D)

    def weight_grads(s, _):
        e = jnp.where(s == 1, c, 1 - c)
        wog[e] = dot(act[s], rows[s, 1].reshape(M, D), 0, 0).astype(BF)
        wig[e] = dot(rows[s, 0].reshape(M, D), hgv[s], 0, 0).astype(BF)
        return 0

    out_copies = [
        pltpu.make_async_copy(wig, wig_hbm, osem.at[0]),
        pltpu.make_async_copy(wog, wog_hbm, osem.at[1]),
    ]

    def r_dev(up, qq):
        if up:
            return z_dev(h, qq + 1) if qq < 3 else z_dev(1 - h, 0)
        return z_dev(h, qq - 1) if qq > 0 else z_dev(1 - h, 3)

    def r_copy(src, up, idx, qq):
        ss = (rsu if up else rsd).at[idx]
        dev = r_dev(up, qq)
        if idx == 8:
            return remote(src, fo, ss, fr.at[0], dev)
        if up and qq == 3 or not up and qq == 0:
            if idx in (4, 7):
                return remote(src, fo, ss, fr.at[0], dev)
            return remote(src, rl, ss, fr.at[1], dev)
        dst, rs = (ru, rur) if up else (rd, rdr)
        return remote(src, dst.at[:, idx], ss, rs.at[idx], dev)

    def r_wait(up, idx):
        dst, rs = (ru, rur) if up else (rd, rdr)
        remote(dst.at[:, idx], dst.at[:, idx], rsu.at[0], rs.at[idx], core_peer).wait_recv()

    def f_wait(k):
        dst = (fo, rl)[k]
        remote(dst, dst, rsu.at[0], fr.at[k], core_peer).wait_recv()

    def begin_reduce(qq):
        up = qq == 0
        for idx in (5, 4, 3, 2, 1) if up else (6, 7, 0, 1, 2):
            r_copy(pv.at[:, idx], up, idx, qq).start()

    def step(qq, up, idx):
        r_wait(up, idx)
        dst = ru if up else rd
        dst[:, idx] = (dst[:, idx].astype(F32) + pv[:, idx].astype(F32)).astype(BF)
        r_copy(dst.at[:, idx], up, idx, qq).start()

    @pl.when(q == 0)
    def _():
        begin_reduce(0)

    @pl.when(q == 3)
    def _():
        begin_reduce(3)

    def finish_reduce(qq, events):
        for up, idx in events:
            step(qq, up, idx)
        if qq in (0, 3):
            f_wait(1)
            r_copy(rl, qq == 0, 8, qq).start()
        total = pv[:, qq].astype(F32)
        if qq > 0:
            r_wait(True, qq)
            total = total + ru[:, qq].astype(F32)
        if qq < 3:
            r_wait(False, qq)
            total = total + rd[:, qq].astype(F32)
        f_wait(0)
        both = jnp.concatenate([total.astype(BF).reshape(64, D), fo[...].reshape(64, D)], axis=0)
        sv2[...] = reorder(perm(order3, True), both).reshape(16, 8, D)
        if qq in (0, 3):
            up = qq == 0
            for idx in (5, 4, 3, 2, 1) if up else (6, 7, 0, 1, 2):
                r_copy(pv.at[:, idx], up, idx, qq).wait_send()
            r_copy(rl, up, 8, qq).wait_send()
        for up, idx in events:
            dst = ru if up else rd
            r_copy(dst.at[:, idx], up, idx, qq).wait_send()

    @pl.when(q == 0)
    def _():
        finish_reduce(0, [(DN, 6), (DN, 7)])

    @pl.when(q == 1)
    def _():
        finish_reduce(1, [(U, 5), (DN, 6), (U, 4), (DN, 7), (U, 3), (DN, 0), (U, 2)])

    @pl.when(q == 2)
    def _():
        finish_reduce(2, [(DN, 6), (U, 5), (DN, 7), (U, 4), (DN, 0), (U, 3), (DN, 1)])

    @pl.when(q == 3)
    def _():
        finish_reduce(3, [(U, 5), (U, 4)])

    back_copies = plane_exchange(sv2, rv2, xs2, xr2)
    lax.fori_loop(0, 2, weight_grads, 0)
    for cp in out_copies:
        cp.start()
    finish(back_copies)
    zs2[...] = reorder(perm(order2, True), rv2[...].reshape(128, D)).reshape(2, 64, D)
    swap2 = remote(zs2.at[1], zr2, core_s.at[1], core_r.at[1], core_peer)
    swap2.start()
    swap2.wait()
    mine = reorder(perm(order1, True), jnp.concatenate([zs2[0], zr2[...]], axis=0))
    slot_out, slot_in = mine[:64], mine[64:]

    cg = dot(g_ref[...], slot_out, 1, 1)
    dg = dot(x_ref[...], slot_in, 1, 1)
    combine, dispatch = comb_v[...], disp_v[...]
    lg = combine * (cg - jnp.sum(cg * combine, axis=1, keepdims=True))
    lg = lg + dispatch * (dg - jnp.sum(dg * dispatch, axis=0, keepdims=True))
    lb = lg.astype(BF)
    part = dot(lb, x_ref[...], 0, 0)
    for p in range(16):
        ra[p] = part[p // 2 * 8 : p // 2 * 8 + 8, p % 2 * 640 : p % 2 * 640 + 640]
    copies = plane_exchange(ra, rb, as1, ar1)
    tg_ref[...] = (dot(dispatch.astype(BF), slot_in) + dot(lb, r_ref[...], 1, 1)).astype(BF)
    finish(copies)
    total = rb[0]
    for p in range(1, 16):
        total = total + rb[p]
    rp[0] = total
    swap3 = remote(rp.at[0], rp.at[1], core_s.at[2], core_r.at[2], core_peer)
    swap3.start()
    swap3.wait()
    zb[z] = rp[0] + rp[1]
    copies = []
    for d, dev, frm in z_peers:
        cp = remote(zb.at[z], zb.at[z], az_s.at[d], az_r.at[d], dev)
        cp.start()
        copies.append(cp)
    for (d, dev, frm), cp in zip(z_peers, copies):
        cp.wait_send()
        remote(zb.at[frm], zb.at[frm], az_s.at[d], az_r.at[d], dev).wait_recv()
    total = zb[0]
    for p in range(1, 8):
        total = total + zb[p]
    rf[...] = total
    rc[xy] = total
    copies = []
    for d, to, frm in xy_peers:
        cp = remote(rf, rc.at[xy], as2.at[d], ar2.at[d], (dp, h * 16 + to))
        cp.start()
        copies.append(cp)
    finish(copies)
    for p in range(8):
        rg_ref[p * 8 : p * 8 + 8, :640] = rc[2 * p]
        rg_ref[p * 8 : p * 8 + 8, 640:] = rc[2 * p + 1]
    for cp in out_copies:
        cp.wait()


def local(tokens, router, w_in, w_out, out_grad):
    vm = pl.BlockSpec(memory_space=pltpu.VMEM)
    anyspace = pl.BlockSpec(memory_space=pl.ANY)
    sem = pltpu.SemaphoreType.DMA
    v = pltpu.VMEM
    block = (2, 32, D)
    scratch = [
        v((2, D, FS), BF), v((2, FS, D), BF), v((2, D, FS), BF), v((2, FS, D), BF),
        v((M, E), F32), v((M, E), F32),
        v((2, 64, D), BF), v((64, D), BF), v((16, 8, D), BF), v((16, 8, D), BF),
        v(block, BF), v(block, BF), v((2, 2, 8, 32, D), BF), v((2, M, FS), BF), v((2, M, FS), BF),
        v((2, M, D), F32), v((2, 8, 32, D), BF), v((2, 8, 32, D), BF), v((2, 8, 32, D), BF),
        v((2, 8, 32, D), BF), v((2, 8, 32, D), BF), v(block, BF), v(block, BF),
        v((2, 64, D), BF), v((64, D), BF), v((16, 8, D), BF), v((16, 8, D), BF),
        v((16, 8, 640), F32), v((16, 8, 640), F32), v((16, 8, 640), F32),
        v((2, 8, 640), F32), v((8, 8, 640), F32), v((8, 640), F32),
        sem((2,)), sem((2,)), sem((3,)), sem((3,)), sem((16,)), sem((16,)), sem((16,)), sem((16,)),
        sem((9,)), sem((9,)), sem((9,)), sem((8,)), sem((8,)), sem((2,)), sem((2,)),
        sem((8,)), sem((8,)), sem((2,)), sem((9,)), sem((9,)),
        sem((16,)), sem((16,)), sem((8,)), sem((8,)), sem((16,)), sem((16,)),
    ]
    tg, rg, wig, wog = pl.pallas_call(
        kernel,
        out_shape=(
            jax.ShapeDtypeStruct((M, D), BF),
            jax.ShapeDtypeStruct((E, D), F32),
            jax.ShapeDtypeStruct((2, D, FS), BF),
            jax.ShapeDtypeStruct((2, FS, D), BF),
        ),
        in_specs=[vm, vm, vm, anyspace, anyspace],
        out_specs=(vm, vm, anyspace, anyspace),
        scratch_shapes=scratch,
        compiler_params=pltpu.CompilerParams(
            collective_id=0, has_side_effects=True, vmem_limit_bytes=56 * 2**20
        ),
        cost_estimate=pl.CostEstimate(
            flops=5 * 10**9, bytes_accessed=13 * 2**20, transcendentals=10**6
        ),
        name="moe_backward",
    )(tokens, out_grad, router, w_in, w_out)
    return tg, rg.T, wig, wog


def solution(mesh):
    both = ("dp", "expert")
    return jax.shard_map(
        local,
        mesh=mesh,
        in_specs=(
            P(both, None), P(), P("expert", None, "dp"), P("expert", "dp", None), P(both, None),
        ),
        out_specs=(P(both, None), P(), P("expert", None, "dp"), P("expert", "dp", None)),
        check_vma=False,
    )
```

time: 485 us -> 119 us (0.25)
  waiting for transfers between devices: 326 us -> 0 us
  Pallas kernels: 0 us -> 107 us
  blocking collectives: 70.8 us -> 0 us
  matrix products: 30 us -> 0 us
  starting transfers between devices: 21.7 us -> 0 us
  between operations: 14 us -> 0.64 us
  local copies, waits for them, and re-layouts: 16.6 us -> 10.5 us
  other arithmetic: 5.36 us -> 0 us
    psum x1 -> x0, waiting for transfers between devices: 241 us -> none  [local(): router_grad = lax.psum(router_part, DP_EXPERT)]
    pallas_call x0 -> x1, Pallas kernels: none -> 107 us  [local(): pl.pallas_call(kernel, out_shape=(jax.ShapeDtypeStruct((M, D), BF), jax.S...]
    reduce_scatter x2 -> x0, waiting for transfers between devices: 61.7 us -> none  [to_owners(): lax.psum_scatter(partial_value, DP, scatter_dimension=0, tiled=True)]
    all_to_all x2 -> x0, blocking collectives: 40.8 us -> none  [to_experts(): lax.all_to_all(slot_rows, 'expert', split_axis=1, concat_axis=0, tiled=True)]
    all_gather x2 -> x0, blocking collectives: 30 us -> none  [gather_in_order(): blocks = lax.all_gather(blocks, axes[k])]
    dot_general x14 -> x0, matrix products: 30 us -> none  [the longest x1 4.46 us: local(): jnp.einsum('ref,efd->red', active_b, w_out, preferred_element_type=jnp.fl...]
    all_to_all x2 -> x0, starting transfers between devices: 21.5 us -> none  [to_owners(): lax.all_to_all(summed, 'expert', split_axis=0, concat_axis=1, tiled=True)]
    all_gather x2 -> x0, waiting for transfers between devices: 15.6 us -> none  [gather_in_order(): blocks = lax.all_gather(blocks, axes[k])]
  transfers between devices with their start and end apart: 7 -> 0, of which waited for: 5 -> 0; matrix products, arithmetic and copies ran while one was open for 6% -> 0% of each run, Pallas kernels for 0% -> 0%
where the time goes in v1:
time: 119 us; the launch traced here: 118 us
  Pallas kernels  107 us (90%)
  local copies, waits for them, and re-layouts  10.5 us (9%)
    pallas_call x1, Pallas kernels, local(): pl.pallas_call(kernel, out_shape=(jax.ShapeDtypeStruct((M, D), BF), jax.S...  107 us
    unnamed x7, local copies, waits for them, and re-layouts  10.5 us

profile of v1, /device:TPU:1, one launch (start us, length us, event | category | flops | bytes accessed | tf_op | source)
XLA Modules:
  0.0 118.1 jit_solution(11920411520212159484)
XLA Ops:
  0.6 1.8 %copy.9.r_ref = bf16[1280,64]{1,0:T(8,128)(2,1)} copy(bf16[1280,64]{0,1:T(8,128)(2,1)} %param.6) | data formatting | bytes 327680 | tf_op args[1]
  2.4 106.9 %moe_backward.1 = (bf16[256,1280]{1,0:T(8,128)(2,1)}, f32[64,1280]{1,0:T(8,128)}, bf16[2,1280,512]{2,1,0:T(8,128)(2,1)}, bf16[2,512,1280]{2,1,0:T(8,128)(2,1)}) custom-call(bf16[256,1280]{1,0:T(8,128)(2,1)} %x_ref.1, bf16[256,1280]{1,0:T(8,128)(2,1)} %g_ref.1, bf16[1280,64]{1,0:T(8,128)(2,1)} %copy.9.r_ref, bf16[2,1280,512]{2,1,0:T(8,128)(2,1)} %wi_hbm.1, ...), custom_call_target="tpu_custom_call" | custom-call | flops 5000000000 | bytes 13631488 | tf_op jit(solution)/shard_map/moe_backward/pallas_call | solution.py:427
  109.4 2.0 %copy.14 = bf16[256,1280]{1,0:T(8,128)(2,1)} copy(bf16[256,1280]{1,0:T(8,128)(2,1)} %get-tuple-element.16) | data formatting | bytes 1310720
  111.3 1.7 %copy.15 = f32[1280,64]{0,1:T(8,128)} copy(f32[1280,64]{0,1:T(8,128)} %bitcast.1) | data formatting | bytes 655360
  113.1 0.0 copy-start
  113.1 3.6 %copy.16 = bf16[2,1280,512]{2,1,0:T(8,128)(2,1)} copy(bf16[2,1280,512]{2,1,0:T(8,128)(2,1)} %get-tuple-element.18) | data formatting | bytes 5242880
  116.6 0.0 copy-done
  116.6 1.5 %copy.17 = bf16[2,512,1280]{2,1,0:T(8,128)(2,1)} copy(bf16[2,512,1280]{2,1,0:T(8,128)(2,1)S(1)} %copy-done) | data formatting | bytes 5242880
Async XLA Ops:
  113.1 3.6 %copy-start = (bf16[2,512,1280]{2,1,0:T(8,128)(2,1)S(1)}, bf16[2,512,1280]{2,1,0:T(8,128)(2,1)}, u32[]{:S(2)}) copy-start(bf16[2,512,1280]{2,1,0:T(8,128)(2,1)} %get-tuple-element.19) | copy-start | bytes 7864324

commit v2 on v0

v2 whole, which is shorter than its diff:
```python
import math

import jax
import jax.numpy as jnp
from jax import lax
from jax.experimental import pallas as pl
from jax.experimental.pallas import tpu as pltpu
from jax.sharding import PartitionSpec as P

MESH = pl.DeviceIdType.MESH
M, D, E, FS = 256, 1280, 64, 512
BF, F32 = jnp.bfloat16, jnp.float32
GELU_C, GELU_A = math.sqrt(2.0 / math.pi), 0.044715


def dot(a, b, ca=1, cb=0):
    return lax.dot_general(a, b, (((ca,), (cb,)), ((), ())), preferred_element_type=F32)


def perm(source, inverse):
    rows = lax.broadcasted_iota(jnp.int32, (64, 64), 1 if inverse else 0)
    cols = lax.broadcasted_iota(jnp.int32, (64, 64), 0 if inverse else 1)
    return (source(rows) == cols).astype(F32).astype(BF)


def reorder(matrix, rows):
    return dot(matrix, rows).astype(BF)


def kernel(
    x_hbm, g_hbm, r_hbm, wi_hbm, wo_hbm,
    tg_ref, rg_ref, wig_hbm, wog_hbm,
    x_ref, g_ref, r_ref, wi, wo, wig, wog,
    comb_v, disp_v,
    zs, zr, sv, rv, ob, rows, act, slope_v, hgv,
    p32, cs, cr, pv, rbuf, fo, zs2, zr2, sv2, rv2,
    ra, rb, rc, zb, rf,
    wsem, osem, core_s, core_r, xs1, xr1, xs2, xr2,
    gr, gsu, gcs, gcr, pcs, pcr,
    rur, rsu, as1, ar1, az_s, az_r, as2, ar2,
):
    dp, ex = lax.axis_index("dp"), lax.axis_index("expert")
    c, q = dp % 2, dp // 2
    h, xy = ex // 16, ex % 16
    y, x = xy // 4, xy % 4
    z = h * 4 + q

    loads = [
        pltpu.make_async_copy(src, dst, wsem.at[k])
        for k, (src, dst) in enumerate(
            [(x_hbm, x_ref), (r_hbm, r_ref), (g_hbm, g_ref), (wi_hbm, wi), (wo_hbm, wo)]
        )
    ]
    for cp in loads:
        cp.start()

    core_peer = (q * 2 + (1 - c), ex)
    xy_peers = []
    for d in (10, 2, 8, 11, 9, 14, 6, 15, 13, 7, 5, 3, 1, 12, 4):
        to = ((y + d // 4) % 4) * 4 + (x + d % 4) % 4
        xy_peers.append((d, to))

    def z_dev(hh, qq):
        return (qq * 2 + c, hh * 16 + xy)

    barrier = pltpu.get_barrier_semaphore()

    def greet(dev):
        pl.semaphore_signal(barrier, inc=1, device_id=dev, device_id_type=MESH)

    for d, to in xy_peers:
        greet((dp, h * 16 + to))
    z_peers = []
    for d in (9, 8, 7, 11, 6, 10, 5, 13, 4, 12, 3, 15, 2, 14, 1):
        zt, ct = (z + d // 2) % 8, (c + d % 2) % 2
        frm = ((z + 8 - d // 2) % 8) * 2 + ct
        z_peers.append((d, (zt % 4 * 2 + ct, zt // 4 * 16 + xy), frm))
        greet(z_peers[-1][1])

    def remote(src, dst, ss, rs, dev):
        return pltpu.make_async_remote_copy(
            src_ref=src, dst_ref=dst, send_sem=ss, recv_sem=rs, device_id=dev, device_id_type=MESH
        )

    def order1(r):
        return (r & 31) * 2 + jnp.where(r < 32, c, 1 - c)

    def order2(r):
        half = jnp.where(((r >> 1) & 1) == 0, h, 1 - h)
        return (r & 1) * 32 + half * 16 + (r >> 2)

    def order3(r):
        return ((r >> 1) & 15) * 4 + (r >> 5) * 2 + (r & 1)

    def swap(t):
        return remote(zs.at[t, 1], zr.at[t], core_s.at[t], core_r.at[t], core_peer)

    def swap2(t):
        return remote(zs2.at[t, 1], zr2.at[t], core_s.at[2 + t], core_r.at[2 + t], core_peer)

    def plane_exchange(src, dst, ss, rs, start):
        copies = []
        for d, to in xy_peers:
            cp = remote(src.at[to], dst.at[xy], ss.at[d], rs.at[d], (dp, h * 16 + to))
            if start:
                cp.start()
            copies.append(cp)
        if start:
            dst[xy] = src[xy]
        return copies

    def finish(copies):
        for cp in copies:
            cp.wait()

    def split(t, local_rows):
        zs[t] = reorder(perm(order1, False), local_rows).reshape(2, 32, D)

    def scatter(t):
        swap(t).wait()
        out = reorder(perm(order2, False), jnp.concatenate([zs[t, 0], zr[t]], axis=0))
        for k in range(16):
            sv[t, k] = out[k * 4 : k * 4 + 4]
        return plane_exchange(sv.at[t], rv.at[t], xs1.at[t], xr1.at[t], True)

    def placed(t, copies):
        finish(copies)
        got = jnp.concatenate([rv[t, k] for k in range(16)], axis=0)
        block = reorder(perm(order3, False), got)
        rows[1, t, q] = block[:32]
        ob[t] = block[32:]

    loads[0].wait()
    loads[1].wait()
    logits = dot(x_ref[...], r_ref[...], 1, 1)
    ed = jnp.exp(logits - jnp.max(logits, axis=0, keepdims=True))
    dispatch = ed / jnp.sum(ed, axis=0, keepdims=True)
    disp_v[...] = dispatch
    split(0, dot(dispatch.astype(BF), x_ref[...], 0, 0).astype(BF))
    pl.semaphore_wait(barrier, 30)
    swap(0).start()
    ec = jnp.exp(logits - jnp.max(logits, axis=1, keepdims=True))
    combine = ec / jnp.sum(ec, axis=1, keepdims=True)
    comb_v[...] = combine
    plane0 = scatter(0)
    loads[2].wait()
    split(1, dot(combine.astype(BF), g_ref[...], 0, 0).astype(BF))
    swap(1).start()
    placed(0, plane0)

    G_BEGIN = [
        [("out", 1, 3), ("out", 1, 1), ("own", 0, 2), ("own", 0, 1)],
        [("out", 1, 3), ("own", 0, 3), ("own", 0, 0), ("own", 0, 2)],
        [("out", 1, 0), ("own", 0, 0), ("own", 0, 3), ("own", 0, 1)],
        [("out", 1, 0), ("out", 1, 2), ("own", 0, 1), ("own", 0, 2)],
    ]
    G_EVENTS = [
        [(7, (1,)), (6, (1, 2)), (1, ()), (2, ()), (3, ()), (4, ()), (5, ())],
        [(3, (0,)), (4, (0,)), (0, ()), (2, ()), (5, (0,)), (7, ()), (6, ())],
        [(0, (3,)), (7, (3,)), (3, ()), (1, ()), (6, (3,)), (4, ()), (5, ())],
        [(4, (2,)), (5, (1, 2)), (2, ()), (1, ()), (0, ()), (7, ()), (6, ())],
    ]
    G_SENDS = [
        G_BEGIN[k] + [(idx, 0, to) for idx, targets in G_EVENTS[k] for to in targets] for k in range(4)
    ]

    def on_plane(body):
        for qq in range(4):
            pl.when(q == qq)(lambda qq=qq: body(qq))

    def place(other, qq):
        return z_dev(1 - h if other else h, qq)

    def g_send(t, qq, k):
        kind, other, to = G_SENDS[qq][k]
        idx = qq if kind == "own" else 4 + qq if kind == "out" else kind
        src = ob.at[t] if kind == "out" else rows.at[1, t, idx]
        return remote(src, rows.at[1, t, idx], gsu.at[t, k], gr.at[t, idx], place(other, to))

    def to_core(t, idx):
        return remote(rows.at[1, t, idx], rows.at[0, t, idx], gcs.at[t, idx], gcr.at[t, idx], core_peer)

    def g_begin(t, qq):
        for k in range(len(G_BEGIN[qq])):
            g_send(t, qq, k).start()
        to_core(t, qq).start()

    def g_events(t, first, last):
        def body(qq):
            k = len(G_BEGIN[qq])
            for n, (idx, targets) in enumerate(G_EVENTS[qq]):
                if first <= n < last:
                    dst = rows.at[1, t, idx]
                    remote(dst, dst, gsu.at[t, 0], gr.at[t, idx], core_peer).wait_recv()
                    for _ in targets:
                        g_send(t, qq, k).start()
                        k += 1
                    to_core(t, idx).start()
                else:
                    k += len(targets)

        on_plane(body)

    def g_sent(t, qq):
        for k in range(len(G_SENDS[qq])):
            g_send(t, qq, k).wait_send()

    on_plane(lambda qq: g_begin(0, qq))
    placed(1, scatter(1))
    g_events(0, 0, 2)
    on_plane(lambda qq: g_begin(1, qq))
    g_events(0, 2, 5)
    g_events(1, 0, 2)
    g_events(0, 5, 7)

    loads[3].wait()
    loads[4].wait()

    def core_sum(t):
        return remote(cs.at[t], cr.at[t], pcs.at[t], pcr.at[t], core_peer)

    def keep_sum(t):
        core_sum(t).wait()
        pv[t] = (p32[...] + cr[t].reshape(M, D).astype(F32)).astype(BF).reshape(8, 32, D)

    def forward(s):
        e = c if s == 1 else 1 - c
        hidden = dot(rows[s, 0].reshape(M, D), wi[e])
        inner = jnp.tanh(GELU_C * (hidden + GELU_A * hidden * hidden * hidden))
        cdf = 0.5 * (1.0 + inner)
        slope_v[s] = cdf + hidden * (
            0.5 * (1.0 - inner * inner) * (GELU_C * (1.0 + 3.0 * GELU_A * hidden * hidden))
        )
        active = (hidden * cdf).astype(BF)
        act[s] = active
        return dot(active, wo[e])

    def give_sum(t, value):
        cs[t] = value.astype(BF).reshape(8, 32, D)
        core_sum(t).start()

    p32[...] = forward(1)
    g_events(1, 2, 4)
    for k in range(8):
        to_core(0, k).wait()
    give_sum(0, forward(0))
    keep_sum(0)

    R_BEGIN = [
        [(5, 0, 1), (4, 0, 1), (3, 0, 1), (2, 0, 2), (1, 0, 1)],
        [(6, 0, 0), (7, 0, 0), (0, 0, 0), (2, 0, 2)],
        [(5, 0, 3), (4, 0, 3), (3, 0, 3), (1, 0, 1)],
        [(6, 0, 2), (7, 0, 2), (0, 0, 2), (1, 0, 1), (2, 0, 2)],
    ]
    R_STEPS = [
        [(7, 1, 3, (1,)), (6, 1, 2, (1, 2))],
        [(5, 0, 3, (0,)), (4, 1, 0, (0,)), (3, 0, 3, (0,))],
        [(6, 0, 0, (3,)), (7, 1, 3, (3,)), (0, 0, 0, (3,))],
        [(4, 1, 0, (2,)), (5, 1, 1, (2, 1))],
    ]
    R_SLOTS = [
        [(7, 1), (6, 1), (6, 2), (0, 1), (0, 2), ("o", 3), ("o", 1)],
        [(5, 0), (4, 0), (3, 0), (1, 0), (1, 2), (1, 3), ("o", 3)],
        [(6, 3), (7, 3), (0, 3), (2, 3), (2, 1), (2, 0), ("o", 0)],
        [(4, 2), (5, 2), (5, 1), (3, 2), (3, 1), ("o", 0), ("o", 2)],
    ]

    def r_send(t, qq, k):
        begin = R_BEGIN[qq]
        if k < len(begin):
            idx, other, to = begin[k]
            src = pv.at[t, idx]
        else:
            idx, other, to, parts = R_STEPS[qq][k - len(begin)]
            src = rbuf.at[t, R_SLOTS[qq].index((idx, parts[0]))]
        slot = R_SLOTS[to].index(("o" if other else idx, qq))
        return remote(src, rbuf.at[t, slot], rsu.at[t, k], rur.at[t, slot], place(other, to))

    def r_wait(t, qq, key):
        slot = R_SLOTS[qq].index(key)
        dst = rbuf.at[t, slot]
        remote(dst, dst, rsu.at[t, 0], rur.at[t, slot], core_peer).wait_recv()
        return slot

    def r_begin(t, qq):
        for k in range(len(R_BEGIN[qq])):
            r_send(t, qq, k).start()

    def r_steps(t, first, last):
        def body(qq):
            for n, (idx, other, to, parts) in list(enumerate(R_STEPS[qq]))[first:last]:
                total = pv[t, idx].astype(F32)
                slots = [r_wait(t, qq, (idx, p)) for p in parts]
                for slot in slots:
                    total = total + rbuf[t, slot].astype(F32)
                rbuf[t, slots[0]] = total.astype(BF)
                r_send(t, qq, len(R_BEGIN[qq]) + n).start()

        on_plane(body)

    def r_sent(t, qq):
        for k in range(len(R_BEGIN[qq]) + len(R_STEPS[qq])):
            r_send(t, qq, k).wait_send()

    def r_total(t, qq):
        total = pv[t, qq].astype(F32)
        outer = None
        for idx, p in R_SLOTS[qq]:
            if idx in (qq, "o"):
                value = rbuf[t, r_wait(t, qq, (idx, p))].astype(F32)
                if idx == qq:
                    total = total + value
                else:
                    outer = value if outer is None else outer + value
        zs2[t, 0] = total.astype(BF)
        fo[t] = outer.astype(BF)

    on_plane(lambda qq: r_begin(0, qq))
    g_events(1, 4, 7)
    for k in range(8):
        to_core(1, k).wait()

    def backward(s):
        e = c if s == 1 else 1 - c
        hg = (dot(rows[s, 1].reshape(M, D), wo[e], 1, 1) * slope_v[s]).astype(BF)
        hgv[s] = hg
        return dot(hg, wi[e], 1, 1)

    p32[...] = backward(1)
    r_steps(0, 0, 1)
    give_sum(1, backward(0))
    r_steps(0, 1, 3)
    keep_sum(1)
    on_plane(lambda qq: r_begin(1, qq))

    def w_out_grad(s, _):
        wog[jnp.where(s == 1, c, 1 - c)] = dot(act[s], rows[s, 1].reshape(M, D), 0, 0).astype(BF)
        return 0

    lax.fori_loop(0, 2, w_out_grad, 0)

    def gathered_back(t):
        both = jnp.concatenate([zs2[t, 0], fo[t]], axis=0)
        out = reorder(perm(order3, True), both)
        for k in range(16):
            sv2[t, k] = out[k * 4 : k * 4 + 4]
        return plane_exchange(sv2.at[t], rv2.at[t], xs2.at[t], xr2.at[t], True)

    def swap_back(t, copies):
        finish(copies)
        got = jnp.concatenate([rv2[t, k] for k in range(16)], axis=0)
        zs2[t] = reorder(perm(order2, True), got).reshape(2, 32, D)
        swap2(t).start()

    def image_rows(t):
        swap2(t).wait()
        return reorder(perm(order1, True), jnp.concatenate([zs2[t, 0], zr2[t]], axis=0))

    on_plane(lambda qq: r_total(0, qq))
    back0 = gathered_back(0)

    r_steps(1, 0, 3)
    swap_back(0, back0)

    def w_in_grad(s, _):
        wig[jnp.where(s == 1, c, 1 - c)] = dot(rows[s, 0].reshape(M, D), hgv[s], 0, 0).astype(BF)
        return 0

    out_copies = [
        pltpu.make_async_copy(wig, wig_hbm, osem.at[0]),
        pltpu.make_async_copy(wog, wog_hbm, osem.at[1]),
    ]
    on_plane(lambda qq: r_total(1, qq))
    back1 = gathered_back(1)
    lax.fori_loop(0, 2, w_in_grad, 0)
    for cp in out_copies:
        cp.start()
    slot_out = image_rows(0)
    cg = dot(g_ref[...], slot_out, 1, 1)
    combine, dispatch = comb_v[...], disp_v[...]
    lg = combine * (cg - jnp.sum(cg * combine, axis=1, keepdims=True))
    swap_back(1, back1)
    slot_in = image_rows(1)

    dg = dot(x_ref[...], slot_in, 1, 1)
    lg = lg + dispatch * (dg - jnp.sum(dg * dispatch, axis=0, keepdims=True))
    lb = lg.astype(BF)
    part = dot(lb, x_ref[...], 0, 0)
    for p in range(16):
        ra[p] = part[p // 2 * 8 : p // 2 * 8 + 8, p % 2 * 640 : p % 2 * 640 + 640].astype(BF)
    copies = plane_exchange(ra, rb, as1, ar1, True)
    tg_ref[...] = (dot(dispatch.astype(BF), slot_in) + dot(lb, r_ref[...])).astype(BF)

    def all_sent(qq):
        for t in range(2):
            g_sent(t, qq)
            r_sent(t, qq)

    on_plane(all_sent)
    finish(copies)
    total = rb[0].astype(F32)
    for p in range(1, 16):
        total = total + rb[p].astype(F32)
    me = z * 2 + c
    zb[me] = total.astype(BF)
    copies = []
    for d, dev, frm in z_peers:
        cp = remote(zb.at[me], zb.at[me], az_s.at[d], az_r.at[d], dev)
        cp.start()
        copies.append((cp, remote(zb.at[frm], zb.at[frm], az_s.at[d], az_r.at[d], dev)))
    for sent, got in copies:
        sent.wait_send()
        got.wait_recv()
    total = zb[0].astype(F32)
    for p in range(1, 16):
        total = total + zb[p].astype(F32)
    rf[...] = total.astype(BF)
    rc[xy] = total.astype(BF)
    copies = []
    for d, to in xy_peers:
        cp = remote(rf, rc.at[xy], as2.at[d], ar2.at[d], (dp, h * 16 + to))
        cp.start()
        copies.append(cp)
    finish(copies)
    rg_ref[...] = rc[...]
    for cp in out_copies:
        cp.wait()


def deliver(tg, rg, wig, wog, tg_out, rg_out, wig_out, wog_out, sem):
    copies = [pltpu.make_async_copy(tg, tg_out, sem.at[8])]
    for k in range(2):
        for half in range(2):
            part = pl.ds(half * (D // 2), D // 2)
            copies.append(pltpu.make_async_copy(wig.at[k, part], wig_out.at[k, part], sem.at[k * 2 + half]))
            part = pl.ds(half * (FS // 2), FS // 2)
            copies.append(
                pltpu.make_async_copy(wog.at[k, part], wog_out.at[k, part], sem.at[4 + k * 2 + half])
            )
    for cp in copies:
        cp.start()
    for p in range(16):
        rg_out[p // 2 * 8 : p // 2 * 8 + 8, p % 2 * 640 : p % 2 * 640 + 640] = rg[p].astype(F32)
    for cp in copies:
        cp.wait()


def local(tokens, router, w_in, w_out, out_grad):
    vm = pl.BlockSpec(memory_space=pltpu.VMEM)
    anyspace = pl.BlockSpec(memory_space=pl.ANY)
    sem = pltpu.SemaphoreType.DMA
    v = pltpu.VMEM
    block, line = (2, 32, D), (2, 8, 32, D)
    scratch = [
        v((M, D), BF), v((M, D), BF), v((E, D), BF),
        v((2, D, FS), BF), v((2, FS, D), BF), v((2, D, FS), BF), v((2, FS, D), BF),
        v((M, E), F32), v((M, E), F32),
        v((2, 2, 32, D), BF), v(block, BF), v((2, 16, 4, D), BF), v((2, 16, 4, D), BF),
        v(block, BF), v((2, 2, 8, 32, D), BF),
        v((2, M, FS), BF), v((2, M, FS), F32), v((2, M, FS), BF),
        v((M, D), F32), v(line, BF), v(line, BF), v(line, BF), v((2, 7, 32, D), BF), v(block, BF),
        v((2, 2, 32, D), BF), v(block, BF), v((2, 16, 4, D), BF), v((2, 16, 4, D), BF),
        v((16, 8, 640), BF), v((16, 8, 640), BF), v((16, 8, 640), BF),
        v((16, 8, 640), BF), v((8, 640), BF),
        sem((5,)), sem((2,)), sem((4,)), sem((4,)),
        sem((2, 16)), sem((2, 16)), sem((2, 16)), sem((2, 16)),
        sem((2, 8)), sem((2, 7)), sem((2, 8)), sem((2, 8)), sem((2,)), sem((2,)),
        sem((2, 7)), sem((2, 7)),
        sem((16,)), sem((16,)), sem((16,)), sem((16,)), sem((16,)), sem((16,)),
    ]
    tg, rg, wig, wog = pl.pallas_call(
        kernel,
        out_shape=(
            jax.ShapeDtypeStruct((M, D), BF),
            jax.ShapeDtypeStruct((16, 8, 640), BF),
            jax.ShapeDtypeStruct((2, D, FS), BF),
            jax.ShapeDtypeStruct((2, FS, D), BF),
        ),
        in_specs=[pl.BlockSpec(memory_space=pltpu.HBM)] * 5,
        out_specs=(vm, vm, anyspace, anyspace),
        scratch_shapes=scratch,
        compiler_params=pltpu.CompilerParams(
            collective_id=0, has_side_effects=True, vmem_limit_bytes=46 * 2**20
        ),
        cost_estimate=pl.CostEstimate(
            flops=5 * 10**9, bytes_accessed=13 * 2**20, transcendentals=10**6
        ),
        name="moe_backward",
    )(tokens, out_grad, router.T, w_in, w_out)
    outs = pl.pallas_call(
        deliver,
        out_shape=(
            jax.ShapeDtypeStruct((M, D), BF),
            jax.ShapeDtypeStruct((E, D), F32),
            jax.ShapeDtypeStruct((2, D, FS), BF),
            jax.ShapeDtypeStruct((2, FS, D), BF),
        ),
        in_specs=[anyspace, vm, anyspace, anyspace],
        out_specs=(anyspace, vm, anyspace, anyspace),
        scratch_shapes=[sem((9,))],
        compiler_params=pltpu.CompilerParams(vmem_limit_bytes=4 * 2**20),
        cost_estimate=pl.CostEstimate(flops=0, bytes_accessed=12 * 2**20, transcendentals=0),
        name="deliver",
    )(tg, rg, wig, wog)
    return outs[0], outs[1].T, outs[2], outs[3]


def solution(mesh):
    both = ("dp", "expert")
    return jax.shard_map(
        local,
        mesh=mesh,
        in_specs=(
            P(both, None), P(), P("expert", None, "dp"), P("expert", "dp", None), P(both, None),
        ),
        out_specs=(P(both, None), P(), P("expert", None, "dp"), P("expert", "dp", None)),
        check_vma=False,
    )
```

time: 485 us -> 107 us (0.22)
  waiting for transfers between devices: 326 us -> 0 us
  Pallas kernels: 0 us -> 103 us
  blocking collectives: 70.8 us -> 0 us
  matrix products: 30 us -> 0 us
  starting transfers between devices: 21.7 us -> 0 us
  local copies, waits for them, and re-layouts: 16.6 us -> 3.08 us
  between operations: 14 us -> 0.65 us
  other arithmetic: 5.36 us -> 0 us
    psum x1 -> x0, waiting for transfers between devices: 241 us -> none  [local(): router_grad = lax.psum(router_part, DP_EXPERT)]
    pallas_call x0 -> x2, Pallas kernels: none -> 103 us  [the longest x1 99.4 us: local(): pl.pallas_call(kernel, out_shape=(jax.ShapeDtypeStruct((M, D), BF), jax.S...]
    reduce_scatter x2 -> x0, waiting for transfers between devices: 61.7 us -> none  [to_owners(): lax.psum_scatter(partial_value, DP, scatter_dimension=0, tiled=True)]
    all_to_all x2 -> x0, blocking collectives: 40.8 us -> none  [to_experts(): lax.all_to_all(slot_rows, 'expert', split_axis=1, concat_axis=0, tiled=True)]
    all_gather x2 -> x0, blocking collectives: 30 us -> none  [gather_in_order(): blocks = lax.all_gather(blocks, axes[k])]
    dot_general x14 -> x0, matrix products: 30 us -> none  [the longest x1 4.46 us: local(): jnp.einsum('ref,efd->red', active_b, w_out, preferred_element_type=jnp.fl...]
    all_to_all x2 -> x0, starting transfers between devices: 21.5 us -> none  [to_owners(): lax.all_to_all(summed, 'expert', split_axis=0, concat_axis=1, tiled=True)]
    all_gather x2 -> x0, waiting for transfers between devices: 15.6 us -> none  [gather_in_order(): blocks = lax.all_gather(blocks, axes[k])]
  transfers between devices with their start and end apart: 7 -> 0, of which waited for: 5 -> 0; matrix products, arithmetic and copies ran while one was open for 6% -> 0% of each run, Pallas kernels for 0% -> 0%
where the time goes in v2:
time: 107 us; the launch traced here: 106 us
  Pallas kernels  103 us (96%)
  local copies, waits for them, and re-layouts  3.08 us (3%)
    pallas_call x1, Pallas kernels, local(): pl.pallas_call(kernel, out_shape=(jax.ShapeDtypeStruct((M, D), BF), jax.S...  99.4 us
    pallas_call x1, Pallas kernels, local(): pl.pallas_call(deliver, out_shape=(jax.ShapeDtypeStruct((M, D), BF), jax....  3.35 us
    unnamed x6, local copies, waits for them, and re-layouts  3.08 us

profile of v2, /device:TPU:1, one launch (start us, length us, event | category | flops | bytes accessed | tf_op | source)
XLA Modules:
  0.0 106.4 jit_solution(5823700664223967056)
XLA Ops:
  0.6 0.0 copy-start
  0.6 1.1 %copy-done = bf16[256,1280]{1,0:T(8,128)(2,1)S(1)} copy-done((bf16[256,1280]{1,0:T(8,128)(2,1)S(1)}, bf16[256,1280]{1,0:T(8,128)(2,1)}, u32[]{:S(2)}) %copy-start) | copy-done | bytes 655384
  1.7 0.0 copy-start.1
  1.7 1.1 %copy-done.1 = bf16[256,1280]{1,0:T(8,128)(2,1)S(1)} copy-done((bf16[256,1280]{1,0:T(8,128)(2,1)S(1)}, bf16[256,1280]{1,0:T(8,128)(2,1)}, u32[]{:S(2)}) %copy-start.1) | copy-done | bytes 655384
  2.8 0.0 copy-start.2
  2.8 0.9 copy-done.2
  3.7 99.4 %moe_backward.1 = (bf16[256,1280]{1,0:T(8,128)(2,1)S(1)}, bf16[16,8,640]{2,1,0:T(8,128)(2,1)S(1)}, bf16[2,1280,512]{2,1,0:T(8,128)(2,1)S(1)}, bf16[2,512,1280]{2,1,0:T(8,128)(2,1)S(1)}) custom-call(bf16[256,1280]{1,0:T(8,128)(2,1)S(1)} %copy-done, bf16[256,1280]{1,0:T(8,128)(2,1)S(1)} %copy-done.1, bf16[64,1280]{1,0:T(8,128)(2,1)S(1)} %bitcast.2, ...), custom_call_target="tpu_custom_call" | custom-call | flops 5000000000 | bytes 13631488 | tf_op jit(solution)/shard_map/moe_backward/pallas_call | solution.py:471
  103.1 3.3 %deliver.1 = (bf16[256,1280]{1,0:T(8,128)(2,1)}, f32[64,1280]{1,0:T(8,128)}, bf16[2,1280,512]{2,1,0:T(8,128)(2,1)}, bf16[2,512,1280]{2,1,0:T(8,128)(2,1)}) custom-call(bf16[256,1280]{1,0:T(8,128)(2,1)S(1)} %get-tuple-element.12.tg, bf16[16,8,640]{2,1,0:T(8,128)(2,1)S(1)} %get-tuple-element.13.rg, bf16[2,1280,512]{2,1,0:T(8,128)(2,1)S(1)} %get-tuple-element.14.wig, ...), custom_call_target="tpu_custom_call" | custom-call | bytes 12582912 | tf_op jit(solution)/shard_map/deliver/pallas_call | solution.py:490
Async XLA Ops:
  0.6 1.1 %copy-start = (bf16[256,1280]{1,0:T(8,128)(2,1)S(1)}, bf16[256,1280]{1,0:T(8,128)(2,1)}, u32[]{:S(2)}) copy-start(bf16[256,1280]{1,0:T(8,128)(2,1)} %x_hbm.1) | copy-start | bytes 1966084
  1.7 1.1 %copy-start.1 = (bf16[256,1280]{1,0:T(8,128)(2,1)S(1)}, bf16[256,1280]{1,0:T(8,128)(2,1)}, u32[]{:S(2)}) copy-start(bf16[256,1280]{1,0:T(8,128)(2,1)} %g_hbm.1) | copy-start | bytes 1966084
  2.8 0.9 copy-start.2

commit v3 on v2

--- a/solution.py
+++ b/solution.py
@@ -34,7 +34,7 @@
     comb_v, disp_v,
     zs, zr, sv, rv, ob, rows, act, slope_v, hgv,
     p32, cs, cr, pv, rbuf, fo, zs2, zr2, sv2, rv2,
-    ra, rb, rc, zb, rf,
+    ra, rb, rc, rp, zb, rf,
     wsem, osem, core_s, core_r, xs1, xr1, xs2, xr2,
     gr, gsu, gcs, gcr, pcs, pcr,
     rur, rsu, as1, ar1, az_s, az_r, as2, ar2,
@@ -51,7 +51,7 @@
             [(x_hbm, x_ref), (r_hbm, r_ref), (g_hbm, g_ref), (wi_hbm, wi), (wo_hbm, wo)]
         )
     ]
-    for cp in loads:
+    for cp in loads[:3]:
         cp.start()
 
     core_peer = (q * 2 + (1 - c), ex)
@@ -70,11 +70,11 @@
 
     for d, to in xy_peers:
         greet((dp, h * 16 + to))
+    greet(core_peer)
     z_peers = []
-    for d in (9, 8, 7, 11, 6, 10, 5, 13, 4, 12, 3, 15, 2, 14, 1):
-        zt, ct = (z + d // 2) % 8, (c + d % 2) % 2
-        frm = ((z + 8 - d // 2) % 8) * 2 + ct
-        z_peers.append((d, (zt % 4 * 2 + ct, zt // 4 * 16 + xy), frm))
+    for d in (4, 3, 5, 2, 6, 1, 7):
+        zt = (z + d) % 8
+        z_peers.append((d, (zt % 4 * 2 + c, zt // 4 * 16 + xy), (z + 8 - d) % 8))
         greet(z_peers[-1][1])
 
     def remote(src, dst, ss, rs, dev):
@@ -132,12 +132,14 @@
 
     loads[0].wait()
     loads[1].wait()
+    for cp in loads[3:]:
+        cp.start()
     logits = dot(x_ref[...], r_ref[...], 1, 1)
     ed = jnp.exp(logits - jnp.max(logits, axis=0, keepdims=True))
     dispatch = ed / jnp.sum(ed, axis=0, keepdims=True)
     disp_v[...] = dispatch
     split(0, dot(dispatch.astype(BF), x_ref[...], 0, 0).astype(BF))
-    pl.semaphore_wait(barrier, 30)
+    pl.semaphore_wait(barrier, 23)
     swap(0).start()
     ec = jnp.exp(logits - jnp.max(logits, axis=1, keepdims=True))
     combine = ec / jnp.sum(ec, axis=1, keepdims=True)
@@ -207,11 +209,11 @@
 
     on_plane(lambda qq: g_begin(0, qq))
     placed(1, scatter(1))
+    on_plane(lambda qq: g_begin(1, qq))
     g_events(0, 0, 2)
-    on_plane(lambda qq: g_begin(1, qq))
     g_events(0, 2, 5)
+    g_events(0, 5, 7)
     g_events(1, 0, 2)
-    g_events(0, 5, 7)
 
     loads[3].wait()
     loads[4].wait()
@@ -401,18 +403,22 @@
     total = rb[0].astype(F32)
     for p in range(1, 16):
         total = total + rb[p].astype(F32)
-    me = z * 2 + c
-    zb[me] = total.astype(BF)
+    half_sum = total.astype(BF)
+    rp[0] = half_sum
+    pair = remote(rp.at[0], rp.at[1], core_s.at[4], core_r.at[4], core_peer)
+    pair.start()
+    pair.wait()
+    zb[z] = (rp[0].astype(F32) + rp[1].astype(F32)).astype(BF)
     copies = []
     for d, dev, frm in z_peers:
-        cp = remote(zb.at[me], zb.at[me], az_s.at[d], az_r.at[d], dev)
+        cp = remote(zb.at[z], zb.at[z], az_s.at[d], az_r.at[d], dev)
         cp.start()
         copies.append((cp, remote(zb.at[frm], zb.at[frm], az_s.at[d], az_r.at[d], dev)))
     for sent, got in copies:
         sent.wait_send()
         got.wait_recv()
     total = zb[0].astype(F32)
-    for p in range(1, 16):
+    for p in range(1, 8):
         total = total + zb[p].astype(F32)
     rf[...] = total.astype(BF)
     rc[xy] = total.astype(BF)
@@ -461,13 +467,14 @@
         v((M, D), F32), v(line, BF), v(line, BF), v(line, BF), v((2, 7, 32, D), BF), v(block, BF),
         v((2, 2, 32, D), BF), v(block, BF), v((2, 16, 4, D), BF), v((2, 16, 4, D), BF),
         v((16, 8, 640), BF), v((16, 8, 640), BF), v((16, 8, 640), BF),
-        v((16, 8, 640), BF), v((8, 640), BF),
-        sem((5,)), sem((2,)), sem((4,)), sem((4,)),
+        v((2, 8, 640), BF), v((8, 8, 640), BF), v((8, 640), BF),
+        sem((5,)), sem((2,)), sem((5,)), sem((5,)),
         sem((2, 16)), sem((2, 16)), sem((2, 16)), sem((2, 16)),
         sem((2, 8)), sem((2, 7)), sem((2, 8)), sem((2, 8)), sem((2,)), sem((2,)),
         sem((2, 7)), sem((2, 7)),
         sem((16,)), sem((16,)), sem((16,)), sem((16,)), sem((16,)), sem((16,)),
     ]
+    operands = (tokens, out_grad, router.T, w_in, w_out)
     tg, rg, wig, wog = pl.pallas_call(
         kernel,
         out_shape=(
@@ -486,7 +493,7 @@
             flops=5 * 10**9, bytes_accessed=13 * 2**20, transcendentals=10**6
         ),
         name="moe_backward",
-    )(tokens, out_grad, router.T, w_in, w_out)
+    )(*(pltpu.with_memory_space_constraint(a, pltpu.HBM) for a in operands))
     outs = pl.pallas_call(
         deliver,
         out_shape=(

time: 107 us -> 100 us (0.935)
  Pallas kernels: 103 us -> 99.6 us
  local copies, waits for them, and re-layouts: 3.08 us -> 0 us
    pallas_call x1, Pallas kernels: 99.4 us -> 96.2 us  [local(): pl.pallas_call(kernel, out_shape=(jax.ShapeDtypeStruct((M, D), BF), jax.S...]
    unnamed x6 -> x0, local copies, waits for them, and re-layouts: 3.08 us -> none
where the time goes in v3:
time: 100 us
  Pallas kernels  99.6 us (100%)
    pallas_call x1, Pallas kernels, local(): pl.pallas_call(kernel, out_shape=(jax.ShapeDtypeStruct((M, D), BF), jax.S...  96.2 us
    pallas_call x1, Pallas kernels, local(): pl.pallas_call(deliver, out_shape=(jax.ShapeDtypeStruct((M, D), BF), jax....  3.35 us

profile of v3, /device:TPU:1, one launch (start us, length us, event | category | flops | bytes accessed | tf_op | source)
XLA Modules:
  0.0 100.2 jit_solution(8990975421946417992)
XLA Ops:
  0.6 96.2 %moe_backward.1 = (bf16[256,1280]{1,0:T(8,128)(2,1)S(1)}, bf16[16,8,640]{2,1,0:T(8,128)(2,1)S(1)}, bf16[2,1280,512]{2,1,0:T(8,128)(2,1)S(1)}, bf16[2,512,1280]{2,1,0:T(8,128)(2,1)S(1)}) custom-call(bf16[256,1280]{1,0:T(8,128)(2,1)} %x_hbm.1, bf16[256,1280]{1,0:T(8,128)(2,1)} %g_hbm.1, bf16[64,1280]{1,0:T(8,128)(2,1)} %bitcast.3, ...), custom_call_target="tpu_custom_call" | custom-call | flops 5000000000 | bytes 13631488 | tf_op jit(solution)/shard_map/moe_backward/pallas_call | solution.py:478
  96.9 3.3 %deliver.1 = (bf16[256,1280]{1,0:T(8,128)(2,1)}, f32[64,1280]{1,0:T(8,128)}, bf16[2,1280,512]{2,1,0:T(8,128)(2,1)}, bf16[2,512,1280]{2,1,0:T(8,128)(2,1)}) custom-call(bf16[256,1280]{1,0:T(8,128)(2,1)S(1)} %get-tuple-element.12.tg, bf16[16,8,640]{2,1,0:T(8,128)(2,1)S(1)} %get-tuple-element.13.rg, bf16[2,1280,512]{2,1,0:T(8,128)(2,1)S(1)} %get-tuple-element.14.wig, ...), custom_call_target="tpu_custom_call" | custom-call | bytes 12582912 | tf_op jit(solution)/shard_map/deliver/pallas_call | solution.py:497

commit v4 on v3

--- a/solution.py
+++ b/solution.py
@@ -242,7 +242,6 @@
         core_sum(t).start()
 
     p32[...] = forward(1)
-    g_events(1, 2, 4)
     for k in range(8):
         to_core(0, k).wait()
     give_sum(0, forward(0))
@@ -318,7 +317,7 @@
         fo[t] = outer.astype(BF)
 
     on_plane(lambda qq: r_begin(0, qq))
-    g_events(1, 4, 7)
+    g_events(1, 2, 7)
     for k in range(8):
         to_core(1, k).wait()
 
@@ -358,10 +357,12 @@
         swap2(t).wait()
         return reorder(perm(order1, True), jnp.concatenate([zs2[t, 0], zr2[t]], axis=0))
 
+
+    r_steps(1, 0, 3)
     on_plane(lambda qq: r_total(0, qq))
     back0 = gathered_back(0)
-
-    r_steps(1, 0, 3)
+    on_plane(lambda qq: r_total(1, qq))
+    back1 = gathered_back(1)
     swap_back(0, back0)
 
     def w_in_grad(s, _):
@@ -372,8 +373,6 @@
         pltpu.make_async_copy(wig, wig_hbm, osem.at[0]),
         pltpu.make_async_copy(wog, wog_hbm, osem.at[1]),
     ]
-    on_plane(lambda qq: r_total(1, qq))
-    back1 = gathered_back(1)
     lax.fori_loop(0, 2, w_in_grad, 0)
     for cp in out_copies:
         cp.start()

time: 100 us -> 100 us (level)
  no operation moved by 1% of the time
where the time goes in v4:
time: 100 us; the launch traced here: 99.9 us
  Pallas kernels  99.3 us (99%)
    pallas_call x1, Pallas kernels, local(): pl.pallas_call(kernel, out_shape=(jax.ShapeDtypeStruct((M, D), BF), jax.S...  95.9 us
    pallas_call x1, Pallas kernels, local(): pl.pallas_call(deliver, out_shape=(jax.ShapeDtypeStruct((M, D), BF), jax....  3.35 us

profile of v4, /device:TPU:1, one launch (start us, length us, event | category | flops | bytes accessed | tf_op | source)
XLA Modules:
  0.0 99.9 jit_solution(11809097415822344432)
XLA Ops:
  0.6 95.9 %moe_backward.1 = (bf16[256,1280]{1,0:T(8,128)(2,1)S(1)}, bf16[16,8,640]{2,1,0:T(8,128)(2,1)S(1)}, bf16[2,1280,512]{2,1,0:T(8,128)(2,1)S(1)}, bf16[2,512,1280]{2,1,0:T(8,128)(2,1)S(1)}) custom-call(bf16[256,1280]{1,0:T(8,128)(2,1)} %x_hbm.1, bf16[256,1280]{1,0:T(8,128)(2,1)} %g_hbm.1, bf16[64,1280]{1,0:T(8,128)(2,1)} %bitcast.3, ...), custom_call_target="tpu_custom_call" | custom-call | flops 5000000000 | bytes 13631488 | tf_op jit(solution)/shard_map/moe_backward/pallas_call | solution.py:477
  96.6 3.3 %deliver.1 = (bf16[256,1280]{1,0:T(8,128)(2,1)}, f32[64,1280]{1,0:T(8,128)}, bf16[2,1280,512]{2,1,0:T(8,128)(2,1)}, bf16[2,512,1280]{2,1,0:T(8,128)(2,1)}) custom-call(bf16[256,1280]{1,0:T(8,128)(2,1)S(1)} %get-tuple-element.12.tg, bf16[16,8,640]{2,1,0:T(8,128)(2,1)S(1)} %get-tuple-element.13.rg, bf16[2,1280,512]{2,1,0:T(8,128)(2,1)S(1)} %get-tuple-element.14.wig, ...), custom_call_target="tpu_custom_call" | custom-call | bytes 12582912 | tf_op jit(solution)/shard_map/deliver/pallas_call | solution.py:496
